TPU v7x, 32 devices: a whole 2x2x4 slice. The times are simulated.
32 devices in a mesh: pair: 16 (over z, y, x), virt: 2 (over core).
Axes of the slice: x: 2, y: 2, z: 4, core: 2. Of those that a mesh axis runs over, the one named last changes fastest.
Arguments:
- amplitudes: bfloat16 [128, 2, 4096], P('pair', 'virt'), may hold values from -6 to 6
- partner: int32 [128], P('pair'), may hold values from 0 to 127, as said below
- integrals: bfloat16 [16, 4096, 4096], P('virt', 'pair'), may hold values from -0.09375 to 0.09375
- pattern: int32 [16], P('virt'), may hold values from 0 to 3, as said below
- owner: int32 [4], replicated, may hold values from 0 to 3, as said below
Outputs:
- ladder: bfloat16 [128, 4, 4096], P('pair', 'virt')
Inputs may be any that keep to these rules, and one draw needn't show every extreme that they name: partner pairs each pair with another one and is its own inverse; the partner of a pair held by index j of pair is held by index j + 16 / 2 modulo 16, that is half the pair axis away. `pattern`: every ab tile pair appears exactly four times in all. owner names every ab tile pair exactly once.
All inputs are finite; a program needn't handle non-finite values.
Results may differ from a plain program's by a relative error of at most 0.0051.
Values may be sent and summed in bfloat16 or wider, within the bound.
No kernel may reach another device: no remote copies, remote signals or barrier semaphores. Data moves between devices by JAX's collectives and lax.ppermute only.
A program may use at most 64 MiB of HBM per device.

v0:
```python
import jax
import jax.numpy as jnp
from jax import lax
from jax.sharding import PartitionSpec as P

TILE = 64


def from_partner(value, axis, stride):
    mask = 2**stride
    pairs = [(source, source ^ mask) for source in range(lax.axis_size(axis))]
    return lax.ppermute(value, axis, pairs)


def symmetrize(plain, mirrored):
    count, width = (plain.shape[0], plain.shape[1])
    flipped = jnp.swapaxes(mirrored.reshape(count, width, TILE, TILE), 2, 3).reshape(plain.shape)
    return (plain.astype(jnp.float32) + flipped.astype(jnp.float32)).astype(jnp.bfloat16)


def shards(amplitudes, partner, integrals, pattern, owner):
    rows = amplitudes.shape[0]
    top_bit = lax.axis_size("pair").bit_length() - 2
    other = from_partner(amplitudes, "pair", top_bit)
    symmetric = symmetrize(amplitudes, jnp.take(other, partner % rows, axis=0))
    piece = lax.all_gather(symmetric, "pair", axis=0, tiled=True)
    flat = piece.reshape(piece.shape[0], -1)
    terms = jnp.einsum("rc,kjc->rkj", flat, integrals, preferred_element_type=jnp.float32)
    selector = (owner[None, :] == pattern[:, None]).astype(jnp.float32)
    spread = jnp.einsum("pkj,ks->psj", terms, selector, precision=lax.Precision.HIGHEST)
    summed = lax.psum_scatter(spread, "virt", scatter_dimension=1, tiled=True)
    result = lax.all_to_all(
        summed.astype(jnp.bfloat16), "pair", split_axis=0, concat_axis=2, tiled=True
    )
    return result


def solution(mesh):
    return jax.shard_map(
        shards,
        mesh=mesh,
        in_specs=(P("pair", "virt", None), P("pair"), P("virt", "pair", None), P("virt"), P()),
        out_specs=P("pair", "virt", None),
        check_vma=False,
    )
```

profile of v0, /device:TPU:0, one launch (start us, length us, event | category | flops | bytes accessed | tf_op | source)
XLA Modules:
  0.0 117.5 jit_solution(4150642547613235944)
XLA Ops:
  6.5 0.0 copy-start.1
  6.5 0.0 copy-start
  6.5 0.0 all-gather.2.cloned.1.call-start
  6.5 4.0 %collective-permute-start = (bf16[8,1,4096]{2,0,1:T(8,128)(2,1)}, bf16[8,1,4096]{2,0,1:T(8,128)(2,1)S(1)}, u32[]{:S(2)}, u32[]{:S(2)}) collective-permute-start(bf16[8,1,4096]{2,0,1:T(8,128)(2,1)} %param.5), channel_id=1, source_target_pairs={{0,16},{2,18},{4,20},{6,22},{8,24},{10,26},{12,28},{14,30},{16,0},... | collective-permute-start | bytes 196616 | tf_op jit(solution)/shard_map/ppermute | solution.py:12
  10.6 0.7 compare_and_fusion
  11.3 3.2 %collective-permute-done = bf16[8,1,4096]{2,0,1:T(8,128)(2,1)S(1)} collective-permute-done((bf16[8,1,4096]{2,0,1:T(8,128)(2,1)}, bf16[8,1,4096]{2,0,1:T(8,128)(2,1)S(1)}, u32[]{:S(2)}, u32[]{:S(2)}) %collective-permute-start) | collective-permute-done | bytes 65568 | tf_op jit(solution)/shard_map/ppermute | solution.py:12
  14.4 0.6 gather_fusion
  15.0 0.2 gather.7
  15.2 0.1 copy.11
  15.3 0.1 convert_bitcast_fusion
  15.4 0.1 reshape.45
  15.6 1.5 %add_convert_fusion = bf16[8,1,4096]{2,0,1:T(8,128)(2,1)} fusion(f32[8,1,4096]{2,0,1:T(8,128)S(1)} %reshape.45, bf16[8,1,4096]{2,0,1:T(8,128)(2,1)} %param.5), kind=kLoop, calls=%fused_computation.6 | loop fusion | flops 98304 | bytes 262144 | tf_op jit(solution)/shard_map/convert_element_type | solution.py:18
  17.0 0.0 all-gather.2.cloned.1.call-update
  17.1 0.0 reduce-scatter.2.cloned.1.call-start
  17.1 56.4 %all-gather.2.cloned.1.call-done = bf16[128,1,4096]{2,0,1:T(8,128)(2,1)} async-done(((bf16[8,1,4096]{2,0,1:T(8,128)(2,1)}), bf16[128,1,4096]{2,0,1:T(8,128)(2,1)}) %all-gather.2.cloned.1.call-update) | async-done | bytes 1048592 | tf_op jit(solution)/shard_map/all_gather | solution.py:26
  73.5 11.8 %fusion = f32[128,8,256]{2,0,1:T(8,128)S(1)} fusion(bf16[8,256,4096]{2,1,0:T(8,128)(2,1)} %param.7, bf16[128,1,4096]{2,0,1:T(8,128)(2,1)} %all-gather.2.cloned.1.call-done), kind=kOutput, calls=%fused_computation.2 | convolution fusion | flops 2147483648 | bytes 18874368 | tf_op jit(solution)/shard_map/rc,kjc->rkj/dot_general | solution.py:28
  85.3 0.0 copy-done.1
  85.3 0.0 copy-done
  85.3 1.2 convolution_bitcast_fusion
  86.5 0.9 copy.13
  87.4 0.0 reduce-scatter.2.cloned.1.call-update
  87.4 6.9 %reduce-scatter.2.cloned.1.call-done = f32[128,2,256]{2,0,1:T(8,128)} async-done(((f32[128,4,256]{2,0,1:T(8,128)}), f32[128,2,256]{2,0,1:T(8,128)}) %reduce-scatter.2.cloned.1.call-update) | async-done | bytes 262160 | tf_op jit(solution)/shard_map/reduce_scatter | solution.py:31
  94.3 1.0 convert_element_type.32
  95.3 0.1 copy.14
  95.4 14.5 %all_to_all.18 = bf16[128,2,256]{2,1,0:T(2,128)(2,1)S(1)} all-to-all(bf16[128,2,256]{2,1,0:T(2,128)(2,1)S(1)} %copy.14), channel_id=1, replica_groups=mesh['pair'=16,'virt'=2] {'pair'}, dimensions={0} | all-to-all | bytes 262144 | tf_op jit(solution)/shard_map/all_to_all | solution.py:32
  109.9 0.8 copy.16
  (1 shorter events, 0.0 us)
Async XLA Ops:
  6.5 78.8 %copy-start.1 = (s32[4]{0:T(128)S(1)}, s32[4]{0:T(128)}, u32[]{:S(2)}) copy-start(s32[4]{0:T(128)} %param.9) | copy-start | bytes 52
  6.5 78.8 %copy-start = (s32[8]{0:T(128)S(1)}, s32[8]{0:T(128)}, u32[]{:S(2)}) copy-start(s32[8]{0:T(128)} %param.8) | copy-start | bytes 100
  6.5 67.0 %all-gather.2.cloned.1.call-start = ((), (), s32[]{:S(2)}) async-start(), calls=%async_computation.2 | async-start | bytes 1114112 | tf_op jit(solution)/shard_map/all_gather | solution.py:26
  6.5 7.9 %collective-permute-start = (bf16[8,1,4096]{2,0,1:T(8,128)(2,1)}, bf16[8,1,4096]{2,0,1:T(8,128)(2,1)S(1)}, u32[]{:S(2)}, u32[]{:S(2)}) collective-permute-start(bf16[8,1,4096]{2,0,1:T(8,128)(2,1)} %param.5), channel_id=1, source_target_pairs={{0,16},{2,18},{4,20},{6,22},{8,24},{10,26},{12,28},{14,30},{16,0},... | collective-permute-start | bytes 196616 | tf_op jit(solution)/shard_map/ppermute | solution.py:12
  17.1 77.2 %reduce-scatter.2.cloned.1.call-start = ((), (), s32[]{:S(2)}) async-start(), calls=%async_computation.3 | async-start | bytes 786432 | tf_op jit(solution)/shard_map/reduce_scatter | solution.py:31
Sparse Core Ops, SparseCore 0:
  17.2 56.3 all-gather.1
  87.5 6.7 reduce-scatter.1
where the time goes:
time: 118 us; the launch traced here: 117 us
  waiting for transfers between devices  66.5 us (56%)
  blocking collectives  14.5 us (12%)
  between operations  13.5 us (11%)
  matrix products  12.9 us (11%)
  starting transfers between devices  4.08 us (3%)
  other arithmetic  3.21 us (3%)
  local copies, waits for them, and re-layouts  2.79 us (2%)
    all_gather x1, waiting for transfers between devices, shards(): piece = lax.all_gather(symmetric, 'pair', axis=0, tiled=True)  56.4 us
    all_to_all x1, blocking collectives, shards(): lax.all_to_all(summed.astype(jnp.bfloat16), 'pair', split_axis=0, concat_...  14.5 us
    dot_general x1, matrix products, shards(): jnp.einsum('rc,kjc->rkj', flat, integrals, preferred_element_type=jnp.flo...  11.8 us
    reduce_scatter x1, waiting for transfers between devices, shards(): summed = lax.psum_scatter(spread, 'virt', scatter_dimension=1, tiled=True)  6.9 us
    ppermute x1, starting transfers between devices, from_partner(): return lax.ppermute(value, axis, pairs)  4.04 us
    ppermute x1, waiting for transfers between devices, from_partner(): return lax.ppermute(value, axis, pairs)  3.18 us
  transfers between devices with their start and end apart: 3, of which 3 were waited for; matrix products, arithmetic and copies ran while one was open for 1% of the time, Pallas kernels for 0%

commit v1 on v0

v1 whole, which is shorter than its diff:
```python
import functools

import jax
import jax.numpy as jnp
from jax import lax
from jax.experimental import pallas as pl
from jax.experimental.pallas import tpu as pltpu
from jax.sharding import PartitionSpec as P

TILE = 64
LANES = 128
CHUNK = 4
SMALL = 2 * 2**20
MEDIUM = 8 * 2**20
LARGE = 28 * 2**20


def exchange(value, axis, mask):
    pairs = [(source, source ^ mask) for source in range(lax.axis_size(axis))]
    return lax.ppermute(value, axis, pairs)


def gather_half(piece, half):
    bits = [1 << n for n in range(half.bit_length() - 1)]
    pieces = {0: piece}
    for mask in sorted(range(1, half), key=lambda mask: bin(mask).count("1") == 2):
        spans = [bit for bit in bits if mask & bit]
        if len(spans) == 2:
            last = spans[0] if spans[1] == 2 * spans[0] else spans[1]
            pieces[mask] = exchange(pieces[mask ^ last], "pair", last)
        else:
            pieces[mask] = exchange(piece, "pair", mask)
    return [pieces[mask] for mask in range(half)]


def listed(index, size):
    inner = 1 << (size.bit_length() - 1) // 2
    away = index // inner - size // inner // 2
    rank = 2 * abs(away) - (away < 0)
    return rank * inner + inner - 1 - index % inner


def rotate(value, axis, step):
    size = lax.axis_size(axis)
    pairs = [(source, (source + step) % size) for source in range(size)]
    return lax.ppermute(value, axis, pairs)


def first_tiles(tiles):
    return jnp.where(early(), tiles, tiles * 5 // 8)


def find_places(pattern, owner, places, filled, share):
    tiles, slots = places.shape[0], filled.shape[0]
    shift = slots - lax.axis_index("virt") * share
    for s in range(slots):
        filled[s] = 0
    for k in range(tiles):
        place = jnp.int32(0)
        for s in range(slots):
            place = jnp.where(owner[s] == pattern[k], s, place)
        places[k] = lax.rem(place + shift, slots)


def stream(k, integrals, stage, arrived):
    return pltpu.make_async_copy(integrals.at[k], stage.at[k], arrived.at[k])


def add_tiles(first, last, integrals, stage, arrived, summed, places, filled):
    step = 32

    def tile(k, carry):
        stream(k, integrals, stage, arrived).wait()
        slot = places[k]
        seen = filled[slot]
        filled[slot] = 1

        def put(i, carry):
            here = pl.ds(pl.multiple_of(i * step, step), step)
            summed[slot, here] = stage[k, here]
            return carry

        def add(i, carry):
            here = pl.ds(pl.multiple_of(i * step, step), step)
            summed[slot, here] += stage[k, here]
            return carry

        @pl.when(seen == 0)
        def store():
            lax.fori_loop(0, summed.shape[1] // step, put, 0)

        @pl.when(seen == 1)
        def later():
            lax.fori_loop(0, summed.shape[1] // step, add, 0)

        return carry

    lax.fori_loop(first, last, tile, 0)


def start_tiles(first, last, integrals, stage, arrived):
    def start(k, carry):
        stream(k, integrals, stage, arrived).start()
        return carry

    lax.fori_loop(first, last, start, 0)


def prepare_kernel(
    share,
    partner_hbm,
    pattern_hbm,
    owner_hbm,
    plain_hbm,
    integrals,
    flipped,
    summed,
    source,
    pick,
    partner,
    pattern,
    owner,
    places,
    filled,
    plain,
    stage,
    by_c,
    by_pair,
    arrived,
    ready,
):
    rows, width = plain.shape
    pairs = width // LANES
    tiles, columns = integrals.shape[:2]
    slots = owner_hbm.shape[0]
    inputs = ((plain_hbm, plain), (pattern_hbm, pattern), (owner_hbm, owner), (partner_hbm, partner))
    copies = [pltpu.make_async_copy(old, new, ready.at[n]) for n, (old, new) in enumerate(inputs)]
    for copy in copies:
        copy.start()
    first = first_tiles(tiles)
    start_tiles(0, first, integrals, stage, arrived)
    copies[0].wait()
    lane = lax.broadcasted_iota(jnp.int32, (rows, LANES), 1)
    for g in range(pairs):
        block = plain[:, g * LANES : (g + 1) * LANES].astype(jnp.float32)
        by_c[(2 * g) * rows : (2 * g + 1) * rows, :] = block
        by_c[(2 * g + 1) * rows : (2 * g + 2) * rows, :] = pltpu.roll(block, TILE, 1)
    for p in range(rows):
        matrix = by_c[pl.ds(p, TILE, stride=rows), :]
        by_pair[p * TILE : (p + 1) * TILE, 0:TILE] = matrix[:, 0:TILE].T
    for g in range(pairs):
        even = by_pair[pl.ds(2 * g, rows, stride=TILE), :]
        odd = by_pair[pl.ds(2 * g + 1, rows, stride=TILE), :]
        flipped[:, g * LANES : (g + 1) * LANES] = jnp.where(lane < TILE, even, pltpu.roll(odd, TILE, 1))
    for copy in copies[1:]:
        copy.wait()
    row = lax.broadcasted_iota(jnp.int32, source.shape, 0)
    chosen = row
    for p in range(rows):
        chosen = jnp.where(row == p, lax.rem(partner[p], rows), chosen)
    source[...] = chosen
    depth = rows * share
    row = lax.broadcasted_iota(jnp.int32, (depth, depth), 0)
    col = lax.broadcasted_iota(jnp.int32, (depth, depth), 1)
    pair, slot = row // share, lax.rem(row, share)
    target = pair
    for p in range(rows):
        target = jnp.where(pair == p, lax.rem(partner[p], rows), target)
    pick[0] = (col == slot * rows + pair).astype(pick.dtype)
    pick[1] = (col == slot * rows + target).astype(pick.dtype)
    find_places(pattern, owner, places, filled, share)
    for s in range(slots):
        present = functools.reduce(jnp.logical_or, [places[k] == s for k in range(tiles)])

        @pl.when(jnp.logical_not(present))
        def empty():
            summed[s] = jnp.zeros(summed.shape[1:], summed.dtype)

    add_tiles(0, first, integrals, stage, arrived, summed, places, filled)


def prepare(partner, pattern, owner, plain, integrals, share):
    rows, width = plain.shape
    tiles, columns = integrals.shape[:2]
    slots = owner.shape[0]
    depth = rows * share
    vmem = pl.BlockSpec(memory_space=pltpu.VMEM)
    inputs = (partner, pattern, owner, plain, integrals)
    return pl.pallas_call(
        functools.partial(prepare_kernel, share),
        out_shape=(
            jax.ShapeDtypeStruct(plain.shape, jnp.float32),
            pltpu.VMEM((slots, columns, width), integrals.dtype),
            jax.ShapeDtypeStruct((rows, LANES), jnp.int32),
            jax.ShapeDtypeStruct((2, depth, depth), jnp.bfloat16),
        ),
        in_specs=[pl.BlockSpec(memory_space=pl.ANY)] * len(inputs),
        out_specs=(vmem, vmem, vmem, vmem),
        scratch_shapes=[
            pltpu.SMEM(partner.shape, jnp.int32),
            pltpu.SMEM(pattern.shape, jnp.int32),
            pltpu.SMEM(owner.shape, jnp.int32),
            pltpu.SMEM(pattern.shape, jnp.int32),
            pltpu.SMEM(owner.shape, jnp.int32),
            pltpu.VMEM(plain.shape, plain.dtype),
            pltpu.VMEM(integrals.shape, integrals.dtype),
            pltpu.VMEM((TILE * rows, LANES), jnp.float32),
            pltpu.VMEM((TILE * rows, LANES), jnp.float32),
            pltpu.SemaphoreType.DMA((tiles,)),
            pltpu.SemaphoreType.DMA((len(inputs) - 1,)),
        ],
        compiler_params=pltpu.CompilerParams(vmem_limit_bytes=LARGE),
        cost_estimate=pl.CostEstimate(flops=integrals.size, bytes_accessed=integrals.size, transcendentals=0),
        name="prepare",
    )(*[in_hbm(value) for value in inputs])


def complete_kernel(
    share, pattern_hbm, owner_hbm, integrals, started, after, summed, pattern, owner, places, filled, stage, arrived, ready
):
    tiles = integrals.shape[0]
    first = first_tiles(tiles)
    copies = [
        pltpu.make_async_copy(pattern_hbm, pattern, ready.at[0]),
        pltpu.make_async_copy(owner_hbm, owner, ready.at[1]),
    ]

    def fill(k, carry):
        filled[places[k]] = 1
        return carry

    @pl.when(first < tiles)
    def other_tiles():
        for copy in copies:
            copy.start()
        start_tiles(first, tiles, integrals, stage, arrived)
        for copy in copies:
            copy.wait()
        find_places(pattern, owner, places, filled, share)
        lax.fori_loop(0, first, fill, 0)
        add_tiles(first, tiles, integrals, stage, arrived, summed, places, filled)


def complete(pattern, owner, integrals, started, after, share):
    tiles, columns, width = integrals.shape
    vmem = pl.BlockSpec(memory_space=pltpu.VMEM)
    anywhere = pl.BlockSpec(memory_space=pl.ANY)
    return pl.pallas_call(
        functools.partial(complete_kernel, share),
        out_shape=pltpu.VMEM(started.shape, started.dtype),
        in_specs=[anywhere, anywhere, anywhere, vmem, anywhere],
        out_specs=vmem,
        scratch_shapes=[
            pltpu.SMEM(pattern.shape, jnp.int32),
            pltpu.SMEM(owner.shape, jnp.int32),
            pltpu.SMEM(pattern.shape, jnp.int32),
            pltpu.SMEM(owner.shape, jnp.int32),
            pltpu.VMEM(integrals.shape, integrals.dtype),
            pltpu.SemaphoreType.DMA((tiles,)),
            pltpu.SemaphoreType.DMA((2,)),
        ],
        input_output_aliases={3: 0},
        compiler_params=pltpu.CompilerParams(vmem_limit_bytes=LARGE),
        cost_estimate=pl.CostEstimate(flops=integrals.size, bytes_accessed=integrals.size, transcendentals=0),
        name="complete",
    )(in_hbm(pattern), in_hbm(owner), in_hbm(integrals), pltpu.with_memory_space_constraint(started, pltpu.VMEM), after)


def in_hbm(value):
    return pltpu.with_memory_space_constraint(value, pltpu.HBM)


def join_kernel(source, flipped, other, out):
    for g in range(other.shape[1] // LANES):
        here = slice(g * LANES, (g + 1) * LANES)
        picked = jnp.take_along_axis(other[:, here].astype(jnp.float32), source[...], axis=0)
        out[:, here] = (flipped[:, here] + picked).astype(out.dtype)


def join(source, flipped, other):
    vmem = pl.BlockSpec(memory_space=pltpu.VMEM)
    return pl.pallas_call(
        join_kernel,
        out_shape=jax.ShapeDtypeStruct(other.shape, other.dtype),
        in_specs=[vmem, vmem, vmem],
        out_specs=vmem,
        compiler_params=pltpu.CompilerParams(vmem_limit_bytes=SMALL),
        cost_estimate=pl.CostEstimate(flops=other.size * 2, bytes_accessed=other.size * 8, transcendentals=0),
        name="join",
    )(source, flipped, other)


def contract_kernel(half, virts, summed, *rest):
    pieces, (weights, theirs, turned) = rest[:half], rest[half:]
    slots, columns, width = summed.shape
    rows = pieces[0].shape[0]
    share = slots // virts
    count = half * rows
    groups = 2 * count // LANES

    def turn(g, carry):
        here = pl.ds(pl.multiple_of(g * LANES, LANES), LANES)
        block = jnp.concatenate([piece[:, here].astype(jnp.float32) for piece in pieces], axis=0).astype(jnp.bfloat16)
        doubled = jnp.concatenate([block, block], axis=0)
        for part in range(groups):
            turned[part, here, :] = doubled[part * LANES : (part + 1) * LANES].T.astype(jnp.float32)
        return carry

    lax.fori_loop(0, width // LANES, turn, 0, unroll=True)
    lane = lax.broadcasted_iota(jnp.int32, (TILE, LANES), 1)
    term = [jnp.zeros((share * columns, 2 * count), jnp.float32) for r in range(1, virts)]
    for first in range(0, width // TILE, CHUNK):
        here = slice(first * TILE, (first + CHUNK) * TILE)
        parts = []
        for part in range(groups):
            values = []
            for c in range(first, first + CHUNK):
                straight = turned[part, c * TILE : (c + 1) * TILE, :]
                back = turned.at[part][pl.ds(c, TILE, stride=TILE), :]
                values.append(jnp.where(lane + part * LANES < count, straight, back))
            parts.append(jnp.concatenate(values, axis=0).astype(weights.dtype))
        chunk = jnp.concatenate(parts, axis=1)
        weights[here, :] = chunk
        for r in range(1, virts):
            tiles = summed[r * share : (r + 1) * share, :, here].reshape(share * columns, CHUNK * TILE)
            term[r - 1] += jnp.dot(tiles, chunk, preferred_element_type=jnp.float32)
    for r in range(1, virts):
        send_home(term[r - 1], theirs.at[r - 1], half, rows, columns)


def early():
    return lax.rem(lax.axis_index("virt"), 2) == 1


def send_home(term, blocks, half, rows, columns):
    place = lax.axis_index("pair")
    inside, upper = lax.rem(place, half), place // half
    share = term.shape[0] // columns
    parts = [term[s * columns : (s + 1) * columns].T.reshape(2 * half, rows, columns) for s in range(share)]
    block = jnp.concatenate(parts, axis=1)
    for m in range(half):
        inner = inside ^ m
        for n, home in ((m, inner + (1 - upper) * half), (half + m, inner + upper * half)):
            blocks[listed(home, 2 * half)] = block[n].astype(blocks.dtype)


def own_kernel(half, rows, share, summed, weights, mine):
    columns, width = summed.shape[1:]
    tiles = summed[0:share].reshape(share * columns, width)
    send_home(jnp.dot(tiles, weights[...], preferred_element_type=jnp.float32), mine, half, rows, columns)


def own(summed, weights, half, rows, share):
    slots, columns, width = summed.shape
    vmem = pl.BlockSpec(memory_space=pltpu.VMEM)
    return pl.pallas_call(
        functools.partial(own_kernel, half, rows, share),
        out_shape=jax.ShapeDtypeStruct((2 * half, share * rows, columns), jnp.float32),
        in_specs=[vmem, vmem],
        out_specs=vmem,
        compiler_params=pltpu.CompilerParams(vmem_limit_bytes=MEDIUM),
        cost_estimate=pl.CostEstimate(
            flops=2 * share * columns * width * weights.shape[1], bytes_accessed=2 * weights.size, transcendentals=0
        ),
        name="own",
    )(pltpu.with_memory_space_constraint(summed, pltpu.VMEM), pltpu.with_memory_space_constraint(weights, pltpu.VMEM))


def contract(summed, pieces, virts):
    slots, columns, width = summed.shape
    half, rows = len(pieces), pieces[0].shape[0]
    count = 2 * half * rows
    share = slots // virts
    vmem = pl.BlockSpec(memory_space=pltpu.VMEM)
    return pl.pallas_call(
        functools.partial(contract_kernel, half, virts),
        out_shape=(
            pltpu.VMEM((width, count), jnp.bfloat16),
            jax.ShapeDtypeStruct((virts - 1, 2 * half, share * rows, columns), jnp.bfloat16),
        ),
        in_specs=[vmem] * (1 + len(pieces)),
        out_specs=(vmem, vmem),
        scratch_shapes=[
            pltpu.VMEM((count // LANES, width, LANES), jnp.float32),
        ],
        compiler_params=pltpu.CompilerParams(vmem_limit_bytes=LARGE),
        cost_estimate=pl.CostEstimate(
            flops=2 * summed.size * count, bytes_accessed=2 * summed.size, transcendentals=0
        ),
        name="contract",
    )(pltpu.with_memory_space_constraint(summed, pltpu.VMEM), *pieces)


def arrange_kernel(pick, received, out):
    sources, depth, columns = received.shape
    rows, share, width = out.shape
    half = sources // 2
    upper = lax.axis_index("pair") // half
    for source in range(sources):
        chosen = pick[jnp.where(upper == source // half, 0, 1)]
        value = jnp.dot(chosen, received[listed(source, sources)], preferred_element_type=jnp.float32)
        here = slice(source * columns, (source + 1) * columns)
        for r in range(rows):
            out[r, :, here] = value[r * share : (r + 1) * share].astype(out.dtype)


def arrange(pick, received, rows, share):
    sources, depth, columns = received.shape
    vmem = pl.BlockSpec(memory_space=pltpu.VMEM)
    return pl.pallas_call(
        arrange_kernel,
        out_shape=jax.ShapeDtypeStruct((rows, share, sources * columns), received.dtype),
        in_specs=[vmem, vmem],
        out_specs=vmem,
        compiler_params=pltpu.CompilerParams(vmem_limit_bytes=SMALL),
        cost_estimate=pl.CostEstimate(flops=2 * received.size, bytes_accessed=4 * received.size, transcendentals=0),
        name="arrange",
    )(pick, received)


def shards(amplitudes, partner, integrals, pattern, owner):
    half = lax.axis_size("pair") // 2
    virts = lax.axis_size("virt")
    rows = amplitudes.shape[0]
    share = owner.shape[0] // virts
    plain = amplitudes.reshape(rows, -1)
    other = exchange(plain, "pair", half)
    flipped, started, source, pick = prepare(partner, pattern, owner, plain, integrals, share)
    pieces = gather_half(join(source, flipped, other), half)
    summed = complete(pattern, owner, integrals, started, pieces[1], share)
    weights, theirs = contract(summed, pieces, virts)
    others = [rotate(theirs[r - 1], "virt", r) for r in range(1, virts)]
    mine = own(summed, weights, half, rows, share)
    for other in others:
        mine = mine + other.astype(jnp.float32)
    order = sorted(range(2 * half), key=lambda index: listed(index, 2 * half))
    received = lax.all_to_all(
        mine.astype(jnp.bfloat16), "pair", split_axis=0, concat_axis=0, tiled=True, axis_index_groups=[order]
    )
    return arrange(pick, received, rows, share)


def solution(mesh):
    return jax.shard_map(
        shards,
        mesh=mesh,
        in_specs=(P("pair", "virt", None), P("pair"), P("virt", "pair", None), P("virt"), P()),
        out_specs=P("pair", "virt", None),
        check_vma=False,
    )
```

time: 118 us -> 36.4 us (0.31)
  waiting for transfers between devices: 66.5 us -> 0.04 us
  between operations: 13.5 us -> 0.11 us
  matrix products: 12.9 us -> 0 us
  Pallas kernels: 0 us -> 12.3 us
  starting transfers between devices: 4.08 us -> 13.7 us
  blocking collectives: 14.5 us -> 10 us
  other arithmetic: 3.21 us -> 0.04 us
  local copies, waits for them, and re-layouts: 2.79 us -> 0 us
    all_gather x1 -> x0, waiting for transfers between devices: 56.4 us -> none  [shards(): piece = lax.all_gather(symmetric, 'pair', axis=0, tiled=True)]
    dot_general x2 -> x0, matrix products: 12.9 us -> none  [the longest x1 11.8 us: shards(): jnp.einsum('rc,kjc->rkj', flat, integrals, preferred_element_type=jnp.flo...]
    pallas_call x0 -> x6, Pallas kernels: none -> 12.3 us  [the longest x1 4.44 us: prepare(): pl.pallas_call(functools.partial(prepare_kernel, share), out_shape=(jax.S...]
    ppermute x1 -> x9, starting transfers between devices: 4.04 us -> 13.7 us  [the longest x8 13.6 us: exchange(): return lax.ppermute(value, axis, pairs)]
    reduce_scatter x1 -> x0, waiting for transfers between devices: 6.9 us -> none  [shards(): summed = lax.psum_scatter(spread, 'virt', scatter_dimension=1, tiled=True)]
    all_to_all x1, blocking collectives: 14.5 us -> 10 us  [shards(): lax.all_to_all(mine.astype(jnp.bfloat16), 'pair', split_axis=0, concat_ax...]
    ppermute x1 -> x9, waiting for transfers between devices: 3.18 us -> 0.04 us  [the longest x8 0.04 us: exchange(): return lax.ppermute(value, axis, pairs)]
    convert_element_type x3 -> x1, other arithmetic: 2.53 us -> 0.04 us  [shards(): mine.astype(jnp.bfloat16)]
  transfers between devices with their start and end apart: 3 -> 9, of which waited for: 3 -> 0; matrix products, arithmetic and copies ran while one was open for 1% -> 0% of each run, Pallas kernels for 0% -> 25%
where the time goes in v1:
time: 36.4 us; the launch traced here: 36.2 us
  starting transfers between devices  13.7 us (38%)
  Pallas kernels  12.3 us (34%)
  blocking collectives  10 us (27%)
    ppermute x8, starting transfers between devices, exchange(): return lax.ppermute(value, axis, pairs)  13.6 us
    all_to_all x1, blocking collectives, shards(): lax.all_to_all(mine.astype(jnp.bfloat16), 'pair', split_axis=0, concat_ax...  10 us
    pallas_call x1, Pallas kernels, prepare(): pl.pallas_call(functools.partial(prepare_kernel, share), out_shape=(jax.S...  4.44 us
    pallas_call x1, Pallas kernels, complete(): pl.pallas_call(functools.partial(complete_kernel, share), out_shape=pltpu...  3.19 us
    pallas_call x1, Pallas kernels, contract(): pl.pallas_call(functools.partial(contract_kernel, half, virts), out_shape...  2.53 us
    pallas_call x1, Pallas kernels, own(): pl.pallas_call(functools.partial(own_kernel, half, rows, share), out_shap...  1.33 us
    pallas_call x1, Pallas kernels, arrange(): pl.pallas_call(arrange_kernel, out_shape=jax.ShapeDtypeStruct((rows, shar...  0.83 us
  transfers between devices with their start and end apart: 9, of which 0 were waited for; matrix products, arithmetic and copies ran while one was open for 0% of the time, Pallas kernels for 25%

profile of v1, /device:TPU:0, one launch (start us, length us, event | category | flops | bytes accessed | tf_op | source)
XLA Modules:
  0.0 36.2 jit_solution(1167027369089603307)
XLA Ops:
  0.0 4.0 %collective-permute-start = (bf16[8,4096]{1,0:T(8,128)(2,1)}, bf16[8,4096]{1,0:T(8,128)(2,1)S(1)}, u32[]{:S(2)}, u32[]{:S(2)}) collective-permute-start(bf16[8,4096]{1,0:T(8,128)(2,1)} %bitcast.3), channel_id=1, source_target_pairs={{0,16},{2,18},{4,20},{6,22},{8,24},{10,26},{12,28},{14,30},{16,0},... | collective-permute-start | bytes 196616 | tf_op jit(solution)/shard_map/ppermute | solution.py:20
  4.0 4.4 %prepare.1 = (f32[8,4096]{1,0:T(8,128)S(1)}, bf16[4,256,4096]{2,1,0:T(8,128)(2,1)S(1)}, s32[8,128]{1,0:T(8,128)S(1)}, bf16[2,16,16]{2,1,0:T(8,128)(2,1)S(1)}) custom-call(s32[8]{0:T(128)} %partner_hbm.1, s32[8]{0:T(128)} %pattern_hbm.3, s32[4]{0:T(128)} %owner_hbm.3, bf16[8,4096]{1,0:T(8,128)(2,1)} %bitcast.4, bf16[8,256,4096]{2,1,0:T(8,128)(2,1)} %integrals.3), custom_call_target="tpu_custom_call" | custom-call | flops 8388608 | bytes 8388608 | tf_op jit(solution)/shard_map/prepare/pallas_call | solution.py:189
  8.5 0.0 collective-permute-done.other
  8.5 1.6 %collective-permute-start.2 = (bf16[8,4096]{1,0:T(8,128)(2,1)S(1)}, bf16[8,4096]{1,0:T(8,128)(2,1)S(1)}, u32[]{:S(2)}, u32[]{:S(2)}) collective-permute-start(bf16[8,4096]{1,0:T(8,128)(2,1)S(1)} %join.1.rest_0_), channel_id=1, source_target_pairs={{0,4},{2,6},{4,0},{6,2},{8,12},{10,14},{12,8},{14,10},{16,20},{18,... | collective-permute-start | bytes 196616 | tf_op jit(solution)/shard_map/ppermute | solution.py:20
  10.1 1.5 %collective-permute-start.1 = (bf16[8,4096]{1,0:T(8,128)(2,1)S(1)}, bf16[8,4096]{1,0:T(8,128)(2,1)S(1)}, u32[]{:S(2)}, u32[]{:S(2)}) collective-permute-start(bf16[8,4096]{1,0:T(8,128)(2,1)S(1)} %join.1.rest_0_), channel_id=1, source_target_pairs={{0,2},{2,0},{4,6},{6,4},{8,10},{10,8},{12,14},{14,12},{16,18},{18,... | collective-permute-start | bytes 196616 | tf_op jit(solution)/shard_map/ppermute | solution.py:20
  11.6 1.6 %collective-permute-start.4 = (bf16[8,4096]{1,0:T(8,128)(2,1)S(1)}, bf16[8,4096]{1,0:T(8,128)(2,1)S(1)}, u32[]{:S(2)}, u32[]{:S(2)}) collective-permute-start(bf16[8,4096]{1,0:T(8,128)(2,1)S(1)} %join.1.rest_0_), channel_id=1, source_target_pairs={{0,8},{2,10},{4,12},{6,14},{8,0},{10,2},{12,4},{14,6},{16,24},{18,... | collective-permute-start | bytes 196616 | tf_op jit(solution)/shard_map/ppermute | solution.py:20
  13.2 0.4 %collective-permute-start.7 = (bf16[8,4096]{1,0:T(8,128)(2,1)S(1)}, bf16[8,4096]{1,0:T(8,128)(2,1)S(1)}, u32[]{:S(2)}, u32[]{:S(2)}) collective-permute-start(bf16[8,4096]{1,0:T(8,128)(2,1)S(1)} %join.1.rest_0_), channel_id=1, source_target_pairs={{0,14},{2,12},{4,10},{6,8},{8,6},{10,4},{12,2},{14,0},{16,30},{18,... | collective-permute-start | bytes 196616 | tf_op jit(solution)/shard_map/ppermute | solution.py:20
  13.5 0.0 collective-permute-done.2.rest_2_
  13.5 1.5 %collective-permute-start.3 = (bf16[8,4096]{1,0:T(8,128)(2,1)S(1)}, bf16[8,4096]{1,0:T(8,128)(2,1)S(1)}, u32[]{:S(2)}, u32[]{:S(2)}) collective-permute-start(bf16[8,4096]{1,0:T(8,128)(2,1)S(1)} %collective-permute-done.2.rest_2_), channel_id=1, source_target_pairs={{0,2},{2,0},{4,6},{6,4},{8,10},{10,8},{12,14},{14,12},{16,18},{18,... | collective-permute-start | bytes 196616 | tf_op jit(solution)/shard_map/ppermute | solution.py:20
  15.0 0.0 collective-permute-done.1.after.rest_1_
  15.1 1.6 %collective-permute-start.5 = (bf16[8,4096]{1,0:T(8,128)(2,1)S(1)}, bf16[8,4096]{1,0:T(8,128)(2,1)S(1)}, u32[]{:S(2)}, u32[]{:S(2)}) collective-permute-start(bf16[8,4096]{1,0:T(8,128)(2,1)S(1)} %collective-permute-done.1.after.rest_1_), channel_id=1, source_target_pairs={{0,8},{2,10},{4,12},{6,14},{8,0},{10,2},{12,4},{14,6},{16,24},{18,... | collective-permute-start | bytes 196616 | tf_op jit(solution)/shard_map/ppermute | solution.py:20
  16.6 0.0 collective-permute-done.4.rest_4_
  16.6 1.5 %collective-permute-start.6 = (bf16[8,4096]{1,0:T(8,128)(2,1)S(1)}, bf16[8,4096]{1,0:T(8,128)(2,1)S(1)}, u32[]{:S(2)}, u32[]{:S(2)}) collective-permute-start(bf16[8,4096]{1,0:T(8,128)(2,1)S(1)} %collective-permute-done.4.rest_4_), channel_id=1, source_target_pairs={{0,4},{2,6},{4,0},{6,2},{8,12},{10,14},{12,8},{14,10},{16,20},{18,... | collective-permute-start | bytes 196616 | tf_op jit(solution)/shard_map/ppermute | solution.py:20
  18.1 3.2 %complete.1.summed = bf16[4,256,4096]{2,1,0:T(8,128)(2,1)S(1)} custom-call(s32[8]{0:T(128)} %pattern_hbm.3, s32[4]{0:T(128)} %owner_hbm.3, bf16[8,256,4096]{2,1,0:T(8,128)(2,1)} %integrals.3, bf16[4,256,4096]{2,1,0:T(8,128)(2,1)S(1)} %get-tuple-element.12.started, ...), custom_call_target="tpu_custom_call", output_to_operand_aliasing={{}: (3, {})} | custom-call | flops 8388608 | bytes 8388608 | tf_op jit(solution)/shard_map/complete/pallas_call | solution.py:248
  21.3 0.0 collective-permute-done.7.rest_7_
  21.4 0.0 collective-permute-done.3.rest_3_
  21.4 0.0 collective-permute-done.5.rest_5_
  21.4 0.0 collective-permute-done.6.rest_6_
  21.4 2.5 %contract.1 = (bf16[4096,128]{1,0:T(8,128)(2,1)S(1)}, bf16[1,16,16,256]{3,2,1,0:T(8,128)(2,1)S(1)}) custom-call(bf16[4,256,4096]{2,1,0:T(8,128)(2,1)S(1)} %complete.1.summed, bf16[8,4096]{1,0:T(8,128)(2,1)S(1)} %join.1.rest_0_, bf16[8,4096]{1,0:T(8,128)(2,1)S(1)} %collective-permute-done.1.after.rest_1_, bf16[8,4096]{1,0:T(8,128)(2,1)S(1)} %collective-permute-done.2.rest_2_, ...), custom_call_target="tpu_custom_call" | custom-call | flops 1073741824 | bytes 8388608 | tf_op jit(solution)/shard_map/contract/pallas_call | solution.py:375
  23.9 0.1 collective-permute-start.8
  24.0 1.3 %own.1 = f32[16,16,256]{2,1,0:T(8,128)S(1)} custom-call(bf16[4,256,4096]{2,1,0:T(8,128)(2,1)S(1)} %complete.1.summed, bf16[4096,128]{1,0:T(8,128)(2,1)S(1)} %get-tuple-element.15.weights), custom_call_target="tpu_custom_call" | custom-call | flops 536870912 | bytes 1048576 | tf_op jit(solution)/shard_map/own/pallas_call | solution.py:356
  25.3 0.0 collective-permute-done.8
  25.4 10.0 %all_to_all.5.received = bf16[16,16,256]{2,1,0:T(8,128)(2,1)S(1)} all-to-all(bf16[16,16,256]{2,1,0:T(8,128)(2,1)S(1)} %add_convert_fusion), channel_id=1, replica_groups={{22,20,18,16,14,12,10,8,30,28,26,24,6,4,2,0},{23,21,19,17,15,13,11,9,31..., dimensions={0} | all-to-all | bytes 262144 | tf_op jit(solution)/shard_map/all_to_all | solution.py:437
  35.4 0.8 %arrange.1 = bf16[8,2,4096]{2,1,0:T(2,128)(2,1)} custom-call(bf16[2,16,16]{2,1,0:T(8,128)(2,1)S(1)} %get-tuple-element.11.pick, bf16[16,16,256]{2,1,0:T(8,128)(2,1)S(1)} %all_to_all.5.received), custom_call_target="tpu_custom_call" | custom-call | flops 131072 | bytes 262144 | tf_op jit(solution)/shard_map/arrange/pallas_call | solution.py:410
  (2 shorter events, 0.1 us)
Async XLA Ops:
  0.0 8.5 %collective-permute-start = (bf16[8,4096]{1,0:T(8,128)(2,1)}, bf16[8,4096]{1,0:T(8,128)(2,1)S(1)}, u32[]{:S(2)}, u32[]{:S(2)}) collective-permute-start(bf16[8,4096]{1,0:T(8,128)(2,1)} %bitcast.3), channel_id=1, source_target_pairs={{0,16},{2,18},{4,20},{6,22},{8,24},{10,26},{12,28},{14,30},{16,0},... | collective-permute-start | bytes 196616 | tf_op jit(solution)/shard_map/ppermute | solution.py:20
  8.5 5.0 %collective-permute-start.2 = (bf16[8,4096]{1,0:T(8,128)(2,1)S(1)}, bf16[8,4096]{1,0:T(8,128)(2,1)S(1)}, u32[]{:S(2)}, u32[]{:S(2)}) collective-permute-start(bf16[8,4096]{1,0:T(8,128)(2,1)S(1)} %join.1.rest_0_), channel_id=1, source_target_pairs={{0,4},{2,6},{4,0},{6,2},{8,12},{10,14},{12,8},{14,10},{16,20},{18,... | collective-permute-start | bytes 196616 | tf_op jit(solution)/shard_map/ppermute | solution.py:20
  10.1 5.0 %collective-permute-start.1 = (bf16[8,4096]{1,0:T(8,128)(2,1)S(1)}, bf16[8,4096]{1,0:T(8,128)(2,1)S(1)}, u32[]{:S(2)}, u32[]{:S(2)}) collective-permute-start(bf16[8,4096]{1,0:T(8,128)(2,1)S(1)} %join.1.rest_0_), channel_id=1, source_target_pairs={{0,2},{2,0},{4,6},{6,4},{8,10},{10,8},{12,14},{14,12},{16,18},{18,... | collective-permute-start | bytes 196616 | tf_op jit(solution)/shard_map/ppermute | solution.py:20
  11.6 5.0 %collective-permute-start.4 = (bf16[8,4096]{1,0:T(8,128)(2,1)S(1)}, bf16[8,4096]{1,0:T(8,128)(2,1)S(1)}, u32[]{:S(2)}, u32[]{:S(2)}) collective-permute-start(bf16[8,4096]{1,0:T(8,128)(2,1)S(1)} %join.1.rest_0_), channel_id=1, source_target_pairs={{0,8},{2,10},{4,12},{6,14},{8,0},{10,2},{12,4},{14,6},{16,24},{18,... | collective-permute-start | bytes 196616 | tf_op jit(solution)/shard_map/ppermute | solution.py:20
  13.2 8.2 %collective-permute-start.7 = (bf16[8,4096]{1,0:T(8,128)(2,1)S(1)}, bf16[8,4096]{1,0:T(8,128)(2,1)S(1)}, u32[]{:S(2)}, u32[]{:S(2)}) collective-permute-start(bf16[8,4096]{1,0:T(8,128)(2,1)S(1)} %join.1.rest_0_), channel_id=1, source_target_pairs={{0,14},{2,12},{4,10},{6,8},{8,6},{10,4},{12,2},{14,0},{16,30},{18,... | collective-permute-start | bytes 196616 | tf_op jit(solution)/shard_map/ppermute | solution.py:20
  13.5 7.8 %collective-permute-start.3 = (bf16[8,4096]{1,0:T(8,128)(2,1)S(1)}, bf16[8,4096]{1,0:T(8,128)(2,1)S(1)}, u32[]{:S(2)}, u32[]{:S(2)}) collective-permute-start(bf16[8,4096]{1,0:T(8,128)(2,1)S(1)} %collective-permute-done.2.rest_2_), channel_id=1, source_target_pairs={{0,2},{2,0},{4,6},{6,4},{8,10},{10,8},{12,14},{14,12},{16,18},{18,... | collective-permute-start | bytes 196616 | tf_op jit(solution)/shard_map/ppermute | solution.py:20
  15.1 6.3 %collective-permute-start.5 = (bf16[8,4096]{1,0:T(8,128)(2,1)S(1)}, bf16[8,4096]{1,0:T(8,128)(2,1)S(1)}, u32[]{:S(2)}, u32[]{:S(2)}) collective-permute-start(bf16[8,4096]{1,0:T(8,128)(2,1)S(1)} %collective-permute-done.1.after.rest_1_), channel_id=1, source_target_pairs={{0,8},{2,10},{4,12},{6,14},{8,0},{10,2},{12,4},{14,6},{16,24},{18,... | collective-permute-start | bytes 196616 | tf_op jit(solution)/shard_map/ppermute | solution.py:20
  16.6 4.7 %collective-permute-start.6 = (bf16[8,4096]{1,0:T(8,128)(2,1)S(1)}, bf16[8,4096]{1,0:T(8,128)(2,1)S(1)}, u32[]{:S(2)}, u32[]{:S(2)}) collective-permute-start(bf16[8,4096]{1,0:T(8,128)(2,1)S(1)} %collective-permute-done.4.rest_4_), channel_id=1, source_target_pairs={{0,4},{2,6},{4,0},{6,2},{8,12},{10,14},{12,8},{14,10},{16,20},{18,... | collective-permute-start | bytes 196616 | tf_op jit(solution)/shard_map/ppermute | solution.py:20
  23.9 1.4 %collective-permute-start.8 = (bf16[16,16,256]{2,1,0:T(8,128)(2,1)S(1)}, bf16[16,16,256]{2,1,0:T(8,128)(2,1)S(1)}, u32[]{:S(2)}, u32[]{:S(2)}) collective-permute-start(bf16[16,16,256]{2,1,0:T(8,128)(2,1)S(1)} %bitcast.2), channel_id=1, source_target_pairs={{0,1},{1,0},{2,3},{3,2},{4,5},{5,4},{6,7},{7,6},{8,9},{9,8},{10,11... | collective-permute-start | bytes 393224 | tf_op jit(solution)/shard_map/ppermute | solution.py:46
